TPU v7x, 32 devices: a whole 2x2x4 slice. The times are simulated.
32 devices in a mesh: layer: 4 (over y, core), tx: 2 (over x), ty: 4 (over z).
Axes of the slice: x: 2, y: 2, z: 4, core: 2. Of those that a mesh axis runs over, the one named last changes fastest.
Arguments:
- layers: float32 [4, 256, 2048], P('layer', 'tx', 'ty'), may hold values from -6 to 6
- wind: int32 [4, 2], P('layer'), may hold values from -128 to 128
- offsets: int32 [4, 9, 2], P('layer'), may hold values from -64 to 64
- weights: bfloat16 [9, 2, 256, 2048], P(None, None, 'tx', 'ty'), may hold values from -0.5 to 0.5
- sub_index: int32 [256, 2048], P('tx', 'ty'), may hold values from -1 to 255, as said below
Outputs:
- slopes: float32 [2, 9, 32, 256], P(None, None, 'tx', 'ty')
Inputs may be any that keep to these rules, and one draw needn't show every extreme that they name: sub_index[i, j] is -1 or j // 8.
All inputs are finite; a program needn't handle non-finite values.
Results may differ from a plain program's by a relative error of at most 0.0003.
Values sent between devices are 32-bit elements; how exact they have to be, the bound alone decides.
A program may use at most 256 MiB of HBM per device.

v0:
```python
import jax
import jax.numpy as jnp
from jax import lax
from jax.sharding import PartitionSpec as P

DIRS = 9
SUB = 8
HMAX = 2
FOOT = 64


def padded(cells, sides, width):
    for axis, dim in sides:
        count = lax.axis_size(axis)
        head = lax.slice_in_dim(cells, 0, width, axis=dim)
        tail = lax.slice_in_dim(cells, cells.shape[dim] - width, cells.shape[dim], axis=dim)
        cells = jnp.concatenate(
            [
                lax.ppermute(tail, axis, [(i, (i + 1) % count) for i in range(count)]),
                cells,
                lax.ppermute(head, axis, [((i + 1) % count, i) for i in range(count)]),
            ],
            axis=dim,
        )
    return cells


def shift_stack(extended, quotient, fraction, out_rows, out_cols):
    margin = HMAX + 1
    field = extended[0]
    start_row = margin - quotient[0, 0]
    start_col = margin - quotient[0, 1]
    corner_aa = lax.dynamic_slice(field, (start_row, start_col), (out_rows, out_cols))
    corner_ab = lax.dynamic_slice(field, (start_row, start_col - 1), (out_rows, out_cols))
    corner_ba = lax.dynamic_slice(field, (start_row - 1, start_col), (out_rows, out_cols))
    corner_bb = lax.dynamic_slice(field, (start_row - 1, start_col - 1), (out_rows, out_cols))
    frow = fraction[0, 0]
    fcol = fraction[0, 1]
    pieces = [
        (1.0 - frow) * ((1.0 - fcol) * corner_aa + fcol * corner_ab)
        + frow * ((1.0 - fcol) * corner_ba + fcol * corner_bb)
    ]
    return jnp.stack(pieces)


def on_device(layers, wind, offsets, weights, sub_index):
    count, rows, cols = layers.shape
    quotient = jnp.floor_divide(wind, 64)
    fraction = (wind - 64 * quotient).astype(jnp.float32) / 64.0
    rimmed = padded(layers, (("tx", 1), ("ty", 2)), HMAX + 1)
    shifted = shift_stack(rimmed, quotient, fraction, rows, cols)
    spread = padded(shifted, (("tx", 1), ("ty", 2)), FOOT)
    live = (sub_index >= 0).astype(jnp.float32)
    results = []
    for d in range(DIRS):
        start_row = FOOT + offsets[0, d, 0]
        start_col = FOOT + offsets[0, d, 1]
        total = lax.dynamic_slice(spread[0], (start_row, start_col), (rows, cols))
        masked = total * live
        terms = weights[d].astype(jnp.float32) * masked[None]
        results.append(terms.reshape(2, rows // SUB, SUB, cols // SUB, SUB).sum(axis=(2, 4)))
    local_slopes = jnp.stack(results, axis=1)
    return lax.psum(local_slopes, "layer")


def solution(mesh):
    placed = (
        P("layer", "tx", "ty"),
        P("layer", None),
        P("layer", None, None),
        P(None, None, "tx", "ty"),
        P("tx", "ty"),
    )
    return jax.shard_map(
        on_device, mesh=mesh, in_specs=placed, out_specs=P(None, None, "tx", "ty"), check_vma=False
    )
```

profile of v0, /device:TPU:0, one launch (start us, length us, event | category | flops | bytes accessed | tf_op | source)
XLA Modules:
  0.0 238.4 jit_solution(12341837292214623267)
XLA Ops:
  15.6 4.1 %collective-permute-start.3 = (f32[1,134,3]{2,1,0:T(8,128)S(1)}, f32[1,134,3]{2,1,0:T(8,128)S(1)}, u32[]{:S(2)}, u32[]{:S(2)}) collective-permute-start(f32[1,134,3]{2,1,0:T(8,128)S(1)} %get-tuple-element.29), channel_id=1, source_target_pairs={{1,0},{2,1},{3,2},{0,3},{5,4},{6,5},{7,6},{4,7},{9,8},{10,9},{11,1... | collective-permute-start | bytes 4832 | tf_op jit(solution)/shard_map/ppermute | solution.py:21
  61.0 7.1 %reshape.200 = f32[2,16,8,64,8]{4,3,2,1,0:T(8,128)} reshape(f32[1,2,128,512]{3,2,1,0:T(8,128)} %get-tuple-element.16) | data formatting | bytes 1048576 | tf_op jit(solution)/shard_map/convert_element_type | solution.py:60
  68.1 7.0 %reshape.201 = f32[2,16,8,64,8]{4,3,2,1,0:T(8,128)} reshape(f32[1,2,128,512]{3,2,1,0:T(8,128)} %get-tuple-element.15) | data formatting | bytes 1048576 | tf_op jit(solution)/shard_map/convert_element_type | solution.py:60
  75.1 7.1 %reshape.202 = f32[2,16,8,64,8]{4,3,2,1,0:T(8,128)} reshape(f32[1,2,128,512]{3,2,1,0:T(8,128)} %get-tuple-element.14) | data formatting | bytes 1048576 | tf_op jit(solution)/shard_map/convert_element_type | solution.py:60
  82.2 6.1 %reshape.203 = f32[2,16,8,64,8]{4,3,2,1,0:T(8,128)} reshape(f32[1,2,128,512]{3,2,1,0:T(8,128)S(1)} %get-tuple-element.13) | data formatting | bytes 1048576 | tf_op jit(solution)/shard_map/convert_element_type | solution.py:60
  88.3 6.2 %reshape.204 = f32[2,16,8,64,8]{4,3,2,1,0:T(8,128)} reshape(f32[1,2,128,512]{3,2,1,0:T(8,128)S(1)} %get-tuple-element.12) | data formatting | bytes 1048576 | tf_op jit(solution)/shard_map/convert_element_type | solution.py:60
  94.5 6.1 %reshape.205 = f32[2,16,8,64,8]{4,3,2,1,0:T(8,128)} reshape(f32[1,2,128,512]{3,2,1,0:T(8,128)S(1)} %get-tuple-element.11) | data formatting | bytes 1048576 | tf_op jit(solution)/shard_map/convert_element_type | solution.py:60
  100.6 6.1 %reshape.206 = f32[2,16,8,64,8]{4,3,2,1,0:T(8,128)} reshape(f32[1,2,128,512]{3,2,1,0:T(8,128)S(1)} %get-tuple-element.10) | data formatting | bytes 1048576 | tf_op jit(solution)/shard_map/convert_element_type | solution.py:60
  106.7 6.1 %reshape.207 = f32[2,16,8,64,8]{4,3,2,1,0:T(8,128)} reshape(f32[1,2,128,512]{3,2,1,0:T(8,128)S(1)} %get-tuple-element.17) | data formatting | bytes 1048576 | tf_op jit(solution)/shard_map/convert_element_type | solution.py:60
  112.8 6.1 %reshape.208 = f32[2,16,8,64,8]{4,3,2,1,0:T(8,128)} reshape(f32[1,2,128,512]{3,2,1,0:T(8,128)S(1)} %get-tuple-element.9) | data formatting | bytes 1048576 | tf_op jit(solution)/shard_map/convert_element_type | solution.py:60
  121.1 3.7 %mul.215 = f32[16,8,64,8]{3,2,1,0:T(8,128)} reshape(f32[128,512]{1,0:T(8,128)S(1)} %get-tuple-element.25) | data formatting | bytes 524288 | tf_op jit(solution)/shard_map/mul | solution.py:60
  124.8 5.9 %multiply_reduce_fusion.8 = f32[2,16,64]{2,1,0:T(8,128)S(1)} fusion(f32[2,16,8,64,8]{4,3,2,1,0:T(8,128)} %reshape.200, f32[16,8,64,8]{3,2,1,0:T(8,128)} %mul.215), kind=kLoop, calls=%fused_computation.8 | loop fusion | flops 260096 | bytes 794624 | tf_op jit(solution)/shard_map/reduce_sum | solution.py:61
  130.7 3.7 %mul.219 = f32[16,8,64,8]{3,2,1,0:T(8,128)} reshape(f32[128,512]{1,0:T(8,128)S(1)} %get-tuple-element.24) | data formatting | bytes 524288 | tf_op jit(solution)/shard_map/mul | solution.py:60
  141.6 3.7 %mul.231 = f32[16,8,64,8]{3,2,1,0:T(8,128)} reshape(f32[128,512]{1,0:T(8,128)S(1)} %get-tuple-element.21) | data formatting | bytes 524288 | tf_op jit(solution)/shard_map/mul | solution.py:60
  148.8 3.7 %mul.239 = f32[16,8,64,8]{3,2,1,0:T(8,128)} reshape(f32[128,512]{1,0:T(8,128)S(1)} %get-tuple-element.19) | data formatting | bytes 524288 | tf_op jit(solution)/shard_map/mul | solution.py:60
  156.1 3.7 %mul.247 = f32[16,8,64,8]{3,2,1,0:T(8,128)} reshape(f32[128,512]{1,0:T(8,128)S(1)} %get-tuple-element.5) | data formatting | bytes 524288 | tf_op jit(solution)/shard_map/mul | solution.py:60
  159.8 6.0 %multiply_reduce_fusion.7 = f32[2,16,64]{2,1,0:T(8,128)S(1)} fusion(f32[2,16,8,64,8]{4,3,2,1,0:T(8,128)} %reshape.201, f32[16,8,64,8]{3,2,1,0:T(8,128)} %mul.219), kind=kLoop, calls=%fused_computation.7 | loop fusion | flops 260096 | bytes 794624 | tf_op jit(solution)/shard_map/reduce_sum | solution.py:61
  165.9 5.0 %multiply_reduce_fusion.6 = f32[2,16,64]{2,1,0:T(8,128)S(1)} fusion(f32[2,16,8,64,8]{4,3,2,1,0:T(8,128)} %reshape.202, f32[16,8,64,8]{3,2,1,0:T(8,128)S(1)} %copy-done.1), kind=kLoop, calls=%fused_computation.6 | loop fusion | flops 260096 | bytes 794624 | tf_op jit(solution)/shard_map/reduce_sum | solution.py:61
  170.9 5.0 %multiply_reduce_fusion.5 = f32[2,16,64]{2,1,0:T(8,128)S(1)} fusion(f32[2,16,8,64,8]{4,3,2,1,0:T(8,128)} %reshape.203, f32[16,8,64,8]{3,2,1,0:T(8,128)S(1)} %copy-done), kind=kLoop, calls=%fused_computation.5 | loop fusion | flops 260096 | bytes 794624 | tf_op jit(solution)/shard_map/reduce_sum | solution.py:61
  176.0 3.8 %multiply_reduce_fusion.4 = f32[2,16,64]{2,1,0:T(8,128)S(1)} fusion(f32[2,16,8,64,8]{4,3,2,1,0:T(8,128)S(1)} %bitcast.107, f32[16,8,64,8]{3,2,1,0:T(8,128)} %mul.231), kind=kLoop, calls=%fused_computation.4 | loop fusion | flops 260096 | bytes 794624 | tf_op jit(solution)/shard_map/reduce_sum | solution.py:61
  179.8 3.8 %multiply_reduce_fusion.3 = f32[2,16,64]{2,1,0:T(8,128)S(1)} fusion(f32[2,16,8,64,8]{4,3,2,1,0:T(8,128)S(1)} %bitcast.105, f32[16,8,64,8]{3,2,1,0:T(8,128)} %mul.235), kind=kLoop, calls=%fused_computation.3 | loop fusion | flops 260096 | bytes 794624 | tf_op jit(solution)/shard_map/reduce_sum | solution.py:61
  183.6 6.0 %multiply_reduce_fusion.2 = f32[2,16,64]{2,1,0:T(8,128)S(1)} fusion(f32[2,16,8,64,8]{4,3,2,1,0:T(8,128)} %reshape.206, f32[16,8,64,8]{3,2,1,0:T(8,128)} %mul.239), kind=kLoop, calls=%fused_computation.2 | loop fusion | flops 260096 | bytes 794624 | tf_op jit(solution)/shard_map/reduce_sum | solution.py:61
  189.6 3.8 %multiply_reduce_fusion.1 = f32[2,16,64]{2,1,0:T(8,128)S(1)} fusion(f32[2,16,8,64,8]{4,3,2,1,0:T(8,128)S(1)} %bitcast.103, f32[16,8,64,8]{3,2,1,0:T(8,128)} %mul.243), kind=kLoop, calls=%fused_computation.1 | loop fusion | flops 260096 | bytes 794624 | tf_op jit(solution)/shard_map/reduce_sum | solution.py:61
  197.8 32.3 %all-reduce.2.cloned.1.call-done = f32[2,9,16,64]{3,2,1,0:T(8,128)} async-done(((f32[2,9,16,64]{3,2,1,0:T(8,128)}), f32[2,9,16,64]{3,2,1,0:T(8,128)}) %all-reduce.2.cloned.1.call-update) | async-done | bytes 73744 | tf_op jit(solution)/shard_map/psum | solution.py:63
  (80 shorter events, 45.0 us)
Async XLA Ops:
  6.5 32.0 %copy-start.6 = (s32[1,9,2]{1,2,0:T(2,128)S(1)}, s32[1,9,2]{1,2,0:T(2,128)}, u32[]{:S(2)}) copy-start(s32[1,9,2]{1,2,0:T(2,128)} %param.7) | copy-start | bytes 220
  6.5 223.5 %all-reduce.2.cloned.1.call-start = ((), (), s32[]{:S(2)}) async-start(), calls=%async_computation | async-start | bytes 294912 | tf_op jit(solution)/shard_map/psum | solution.py:63
  7.3 7.3 %collective-permute-start.1 = (f32[1,3,512]{2,1,0:T(4,128)S(1)}, f32[1,3,512]{2,1,0:T(4,128)S(1)}, u32[]{:S(2)}, u32[]{:S(2)}) collective-permute-start(f32[1,3,512]{2,1,0:T(4,128)S(1)} %get-tuple-element.33), channel_id=1, source_target_pairs={{4,0},{0,4},{5,1},{1,5},{6,2},{2,6},{7,3},{3,7},{12,8},{8,12},{13,... | collective-permute-start | bytes 18440 | tf_op jit(solution)/shard_map/ppermute | solution.py:21
  10.2 4.4 %collective-permute-start = (f32[1,3,512]{2,1,0:T(4,128)S(1)}, f32[1,3,512]{2,1,0:T(4,128)S(1)}, u32[]{:S(2)}, u32[]{:S(2)}) collective-permute-start(f32[1,3,512]{2,1,0:T(4,128)S(1)} %get-tuple-element.32), channel_id=1, source_target_pairs={{0,4},{4,0},{1,5},{5,1},{2,6},{6,2},{3,7},{7,3},{8,12},{12,8},{9,1... | collective-permute-start | bytes 18440 | tf_op jit(solution)/shard_map/ppermute | solution.py:19
  15.6 7.8 %collective-permute-start.3 = (f32[1,134,3]{2,1,0:T(8,128)S(1)}, f32[1,134,3]{2,1,0:T(8,128)S(1)}, u32[]{:S(2)}, u32[]{:S(2)}) collective-permute-start(f32[1,134,3]{2,1,0:T(8,128)S(1)} %get-tuple-element.29), channel_id=1, source_target_pairs={{1,0},{2,1},{3,2},{0,3},{5,4},{6,5},{7,6},{4,7},{9,8},{10,9},{11,1... | collective-permute-start | bytes 4832 | tf_op jit(solution)/shard_map/ppermute | solution.py:21
  19.7 6.1 %collective-permute-start.2 = (f32[1,134,3]{2,1,0:T(8,128)S(1)}, f32[1,134,3]{2,1,0:T(8,128)S(1)}, u32[]{:S(2)}, u32[]{:S(2)}) collective-permute-start(f32[1,134,3]{2,1,0:T(8,128)S(1)} %get-tuple-element.28), channel_id=1, source_target_pairs={{0,1},{1,2},{2,3},{3,0},{4,5},{5,6},{6,7},{7,4},{8,9},{9,10},{10,1... | collective-permute-start | bytes 4832 | tf_op jit(solution)/shard_map/ppermute | solution.py:19
  28.6 5.3 %collective-permute-start.5 = (f32[1,64,512]{2,1,0:T(8,128)S(1)}, f32[1,64,512]{2,1,0:T(8,128)S(1)}, u32[]{:S(2)}, u32[]{:S(2)}) collective-permute-start(f32[1,64,512]{2,1,0:T(8,128)S(1)} %get-tuple-element.31), channel_id=1, source_target_pairs={{4,0},{0,4},{5,1},{1,5},{6,2},{2,6},{7,3},{3,7},{12,8},{8,12},{13,... | collective-permute-start | bytes 393224 | tf_op jit(solution)/shard_map/ppermute | solution.py:21
  30.1 5.0 %collective-permute-start.4 = (f32[1,64,512]{2,1,0:T(8,128)S(1)}, f32[1,64,512]{2,1,0:T(8,128)S(1)}, u32[]{:S(2)}, u32[]{:S(2)}) collective-permute-start(f32[1,64,512]{2,1,0:T(8,128)S(1)} %get-tuple-element.30), channel_id=1, source_target_pairs={{0,4},{4,0},{1,5},{5,1},{2,6},{6,2},{3,7},{7,3},{8,12},{12,8},{9,1... | collective-permute-start | bytes 393224 | tf_op jit(solution)/shard_map/ppermute | solution.py:19
  35.1 0.6 copy-start.2
  36.5 82.4 %collective-permute-start.7 = (f32[1,256,64]{2,1,0:T(8,128)}, f32[1,256,64]{2,1,0:T(8,128)}, u32[]{:S(2)}, u32[]{:S(2)}) collective-permute-start(f32[1,256,64]{2,1,0:T(8,128)} %get-tuple-element.27), channel_id=1, source_target_pairs={{1,0},{2,1},{3,2},{0,3},{5,4},{6,5},{7,6},{4,7},{9,8},{10,9},{11,1... | collective-permute-start | bytes 196616 | tf_op jit(solution)/shard_map/ppermute | solution.py:21
  38.4 80.6 %collective-permute-start.6 = (f32[1,256,64]{2,1,0:T(8,128)}, f32[1,256,64]{2,1,0:T(8,128)}, u32[]{:S(2)}, u32[]{:S(2)}) collective-permute-start(f32[1,256,64]{2,1,0:T(8,128)} %get-tuple-element.26), channel_id=1, source_target_pairs={{0,1},{1,2},{2,3},{3,0},{4,5},{5,6},{6,7},{7,4},{8,9},{9,10},{10,1... | collective-permute-start | bytes 196616 | tf_op jit(solution)/shard_map/ppermute | solution.py:19
  106.7 12.2 %copy-start.3 = (f32[1,64,512]{2,1,0:T(8,128)S(1)}, f32[1,64,512]{2,1,0:T(8,128)}, u32[]{:S(2)}) copy-start(f32[1,64,512]{2,1,0:T(8,128)} %copy-done.2) | copy-start | bytes 393220
  106.7 13.5 %copy-start.4 = (s32[128,512]{1,0:T(8,128)S(1)}, s32[128,512]{1,0:T(8,128)}, u32[]{:S(2)}) copy-start(s32[128,512]{1,0:T(8,128)} %param.9) | copy-start | bytes 786436
  159.8 6.0 %copy-start.1 = (f32[16,8,64,8]{3,2,1,0:T(8,128)S(1)}, f32[16,8,64,8]{3,2,1,0:T(8,128)}, u32[]{:S(2)}) copy-start(f32[16,8,64,8]{3,2,1,0:T(8,128)} %mul.223) | copy-start | bytes 786436
  165.8 5.1 %copy-start = (f32[16,8,64,8]{3,2,1,0:T(8,128)S(1)}, f32[16,8,64,8]{3,2,1,0:T(8,128)}, u32[]{:S(2)}) copy-start(f32[16,8,64,8]{3,2,1,0:T(8,128)} %mul.227) | copy-start | bytes 786436
  165.8 10.1 %slice-start.6 = ((s8[8388608]{0:T(1024)(128)(4,1)}), s8[4194304]{0:T(1024)(128)(4,1)S(1)}, s32[]{:S(2)}) async-start(s8[8388608]{0:T(1024)(128)(4,1)} %bitcast.106), calls=%async_computation.7 | async-start | bytes 8388608
  170.9 5.1 %slice-start.7 = ((s8[8388608]{0:T(1024)(128)(4,1)}), s8[4194304]{0:T(1024)(128)(4,1)S(1)}, s32[]{:S(2)}) async-start(s8[8388608]{0:T(1024)(128)(4,1)} %bitcast.106), calls=%async_computation.8 | async-start | bytes 8388608
  170.9 8.9 %slice-start.4 = ((s8[8388608]{0:T(1024)(128)(4,1)}), s8[4194304]{0:T(1024)(128)(4,1)S(1)}, s32[]{:S(2)}) async-start(s8[8388608]{0:T(1024)(128)(4,1)} %bitcast.104), calls=%async_computation.5 | async-start | bytes 8388608
  176.0 3.8 %slice-start.5 = ((s8[8388608]{0:T(1024)(128)(4,1)}), s8[4194304]{0:T(1024)(128)(4,1)S(1)}, s32[]{:S(2)}) async-start(s8[8388608]{0:T(1024)(128)(4,1)} %bitcast.104), calls=%async_computation.6 | async-start | bytes 8388608
  179.8 9.8 %slice-start.2 = ((s8[8388608]{0:T(1024)(128)(4,1)}), s8[4194304]{0:T(1024)(128)(4,1)S(1)}, s32[]{:S(2)}) async-start(s8[8388608]{0:T(1024)(128)(4,1)} %bitcast.102), calls=%async_computation.3 | async-start | bytes 8388608
  183.6 6.0 %slice-start.3 = ((s8[8388608]{0:T(1024)(128)(4,1)}), s8[4194304]{0:T(1024)(128)(4,1)S(1)}, s32[]{:S(2)}) async-start(s8[8388608]{0:T(1024)(128)(4,1)} %bitcast.102), calls=%async_computation.4 | async-start | bytes 8388608
  183.6 9.9 %slice-start = ((s8[8388608]{0:T(1024)(128)(4,1)}), s8[4194304]{0:T(1024)(128)(4,1)S(1)}, s32[]{:S(2)}) async-start(s8[8388608]{0:T(1024)(128)(4,1)} %bitcast.100), calls=%async_computation.1 | async-start | bytes 8388608
  189.6 3.8 %slice-start.1 = ((s8[8388608]{0:T(1024)(128)(4,1)}), s8[4194304]{0:T(1024)(128)(4,1)S(1)}, s32[]{:S(2)}) async-start(s8[8388608]{0:T(1024)(128)(4,1)} %bitcast.100), calls=%async_computation.2 | async-start | bytes 8388608
  197.1 0.7 copy-start.5
Sparse Core Ops, SparseCore 0:
  197.9 32.0 all-reduce.1
where the time goes:
time: 239 us; the launch traced here: 238 us
  local copies, waits for them, and re-layouts  96.4 us (40%)
  other arithmetic  53.4 us (22%)
  between operations  41.5 us (17%)
  waiting for transfers between devices  35.9 us (15%)
  starting transfers between devices  11.2 us (5%)
    convert_element_type x9, local copies, waits for them, and re-layouts, on_device(): terms = weights[d].astype(jnp.float32) * masked[None]  57.9 us
    reduce_sum x9, other arithmetic, on_device(): terms.reshape(2, rows // SUB, SUB, cols // SUB, SUB).sum(axis=(2, 4))  42.9 us
    mul x9, local copies, waits for them, and re-layouts, on_device(): terms = weights[d].astype(jnp.float32) * masked[None]  32.8 us
    psum x1, waiting for transfers between devices, on_device(): return lax.psum(local_slopes, 'layer')  32.3 us
    ppermute x4, starting transfers between devices, padded(): lax.ppermute(head, axis, [((i + 1) % count, i) for i in range(count)])  10.5 us
  transfers between devices with their start and end apart: 9, of which 3 were waited for; matrix products, arithmetic and copies ran while one was open for 27% of the time, Pallas kernels for 0%

commit v1 on v0

--- a/solution.py
+++ b/solution.py
@@ -1,3 +1,4 @@
+import functools
 import jax
 import jax.numpy as jnp
 from jax import lax
@@ -7,6 +8,14 @@
 SUB = 8
 HMAX = 2
 FOOT = 64
+
+
+def group_positions(z, ax_name):
+    parts_out = jnp.sum(lax.all_gather(z, ax_name), axis=0)
+    return parts_out
+
+
+_pair_slot = functools.partial(group_positions, ax_name="layer")
 
 
 def padded(cells, sides, width):
@@ -60,7 +69,7 @@
         terms = weights[d].astype(jnp.float32) * masked[None]
         results.append(terms.reshape(2, rows // SUB, SUB, cols // SUB, SUB).sum(axis=(2, 4)))
     local_slopes = jnp.stack(results, axis=1)
-    return lax.psum(local_slopes, "layer")
+    return _pair_slot(local_slopes)
 
 
 def solution(mesh):

time: 239 us -> 200 us (0.84)
  waiting for transfers between devices: 35.9 us -> 3.61 us
  between operations: 41.5 us -> 28.2 us
  blocking collectives: 0 us -> 7.54 us
    psum x1 -> x0, waiting for transfers between devices: 32.3 us -> none  [on_device(): return lax.psum(local_slopes, 'layer')]
    all_gather x0 -> x1, blocking collectives: none -> 7.54 us  [group_positions(): parts_out = jnp.sum(lax.all_gather(z, ax_name), axis=0)]
  transfers between devices with their start and end apart: 9 -> 8, of which waited for: 3 -> 2; matrix products, arithmetic and copies ran while one was open for 27% -> 32% of each run, Pallas kernels for 0% -> 0%
where the time goes in v1:
time: 200 us; the launch traced here: 199 us
  local copies, waits for them, and re-layouts  94.8 us (47%)
  other arithmetic  53.5 us (27%)
  between operations  28.2 us (14%)
  starting transfers between devices  11.2 us (6%)
  blocking collectives  7.54 us (4%)
  waiting for transfers between devices  3.61 us (2%)
    convert_element_type x9, local copies, waits for them, and re-layouts, on_device(): terms = weights[d].astype(jnp.float32) * masked[None]  57.8 us
    reduce_sum x9, other arithmetic, on_device(): terms.reshape(2, rows // SUB, SUB, cols // SUB, SUB).sum(axis=(2, 4))  42.9 us
    mul x9, local copies, waits for them, and re-layouts, on_device(): terms = weights[d].astype(jnp.float32) * masked[None]  32.9 us
    ppermute x4, starting transfers between devices, padded(): lax.ppermute(head, axis, [((i + 1) % count, i) for i in range(count)])  10.5 us
    all_gather x1, blocking collectives, group_positions(): parts_out = jnp.sum(lax.all_gather(z, ax_name), axis=0)  7.54 us
  transfers between devices with their start and end apart: 8, of which 2 were waited for; matrix products, arithmetic and copies ran while one was open for 32% of the time, Pallas kernels for 0%

profile of v1, /device:TPU:0, one launch (start us, length us, event | category | flops | bytes accessed | tf_op | source)
XLA Modules:
  0.0 198.9 jit_solution(3416383736022666705)
XLA Ops:
  9.1 4.1 %collective-permute-start.3 = (f32[1,134,3]{2,1,0:T(8,128)S(1)}, f32[1,134,3]{2,1,0:T(8,128)S(1)}, u32[]{:S(2)}, u32[]{:S(2)}) collective-permute-start(f32[1,134,3]{2,1,0:T(8,128)S(1)} %get-tuple-element.29), channel_id=1, source_target_pairs={{1,0},{2,1},{3,2},{0,3},{5,4},{6,5},{7,6},{4,7},{9,8},{10,9},{11,1... | collective-permute-start | bytes 4832 | tf_op jit(solution)/shard_map/ppermute | solution.py:30
  54.6 7.1 %reshape.200 = f32[2,16,8,64,8]{4,3,2,1,0:T(8,128)} reshape(f32[1,2,128,512]{3,2,1,0:T(8,128)} %get-tuple-element.16) | data formatting | bytes 1048576 | tf_op jit(solution)/shard_map/convert_element_type | solution.py:69
  61.7 7.0 %reshape.201 = f32[2,16,8,64,8]{4,3,2,1,0:T(8,128)} reshape(f32[1,2,128,512]{3,2,1,0:T(8,128)} %get-tuple-element.15) | data formatting | bytes 1048576 | tf_op jit(solution)/shard_map/convert_element_type | solution.py:69
  68.7 7.0 %reshape.202 = f32[2,16,8,64,8]{4,3,2,1,0:T(8,128)} reshape(f32[1,2,128,512]{3,2,1,0:T(8,128)} %get-tuple-element.14) | data formatting | bytes 1048576 | tf_op jit(solution)/shard_map/convert_element_type | solution.py:69
  75.8 6.1 %reshape.203 = f32[2,16,8,64,8]{4,3,2,1,0:T(8,128)} reshape(f32[1,2,128,512]{3,2,1,0:T(8,128)S(1)} %get-tuple-element.13) | data formatting | bytes 1048576 | tf_op jit(solution)/shard_map/convert_element_type | solution.py:69
  81.9 6.1 %reshape.204 = f32[2,16,8,64,8]{4,3,2,1,0:T(8,128)} reshape(f32[1,2,128,512]{3,2,1,0:T(8,128)S(1)} %get-tuple-element.12) | data formatting | bytes 1048576 | tf_op jit(solution)/shard_map/convert_element_type | solution.py:69
  88.0 6.1 %reshape.205 = f32[2,16,8,64,8]{4,3,2,1,0:T(8,128)} reshape(f32[1,2,128,512]{3,2,1,0:T(8,128)S(1)} %get-tuple-element.11) | data formatting | bytes 1048576 | tf_op jit(solution)/shard_map/convert_element_type | solution.py:69
  94.1 6.1 %reshape.206 = f32[2,16,8,64,8]{4,3,2,1,0:T(8,128)} reshape(f32[1,2,128,512]{3,2,1,0:T(8,128)S(1)} %get-tuple-element.10) | data formatting | bytes 1048576 | tf_op jit(solution)/shard_map/convert_element_type | solution.py:69
  100.2 6.1 %reshape.207 = f32[2,16,8,64,8]{4,3,2,1,0:T(8,128)} reshape(f32[1,2,128,512]{3,2,1,0:T(8,128)S(1)} %get-tuple-element.17) | data formatting | bytes 1048576 | tf_op jit(solution)/shard_map/convert_element_type | solution.py:69
  106.3 6.1 %reshape.208 = f32[2,16,8,64,8]{4,3,2,1,0:T(8,128)} reshape(f32[1,2,128,512]{3,2,1,0:T(8,128)S(1)} %get-tuple-element.9) | data formatting | bytes 1048576 | tf_op jit(solution)/shard_map/convert_element_type | solution.py:69
  114.6 3.7 %mul.215 = f32[16,8,64,8]{3,2,1,0:T(8,128)} reshape(f32[128,512]{1,0:T(8,128)S(1)} %get-tuple-element.25) | data formatting | bytes 524288 | tf_op jit(solution)/shard_map/mul | solution.py:69
  118.3 5.9 %multiply_reduce_fusion.8 = f32[2,16,64]{2,1,0:T(8,128)S(1)} fusion(f32[2,16,8,64,8]{4,3,2,1,0:T(8,128)} %reshape.200, f32[16,8,64,8]{3,2,1,0:T(8,128)} %mul.215), kind=kLoop, calls=%fused_computation.8 | loop fusion | flops 260096 | bytes 794624 | tf_op jit(solution)/shard_map/reduce_sum | solution.py:70
  124.2 3.7 %mul.219 = f32[16,8,64,8]{3,2,1,0:T(8,128)} reshape(f32[128,512]{1,0:T(8,128)S(1)} %get-tuple-element.24) | data formatting | bytes 524288 | tf_op jit(solution)/shard_map/mul | solution.py:69
  135.1 3.7 %mul.231 = f32[16,8,64,8]{3,2,1,0:T(8,128)} reshape(f32[128,512]{1,0:T(8,128)S(1)} %get-tuple-element.21) | data formatting | bytes 524288 | tf_op jit(solution)/shard_map/mul | solution.py:69
  142.4 3.7 %mul.239 = f32[16,8,64,8]{3,2,1,0:T(8,128)} reshape(f32[128,512]{1,0:T(8,128)S(1)} %get-tuple-element.19) | data formatting | bytes 524288 | tf_op jit(solution)/shard_map/mul | solution.py:69
  149.7 3.7 %mul.247 = f32[16,8,64,8]{3,2,1,0:T(8,128)} reshape(f32[128,512]{1,0:T(8,128)S(1)} %get-tuple-element.5) | data formatting | bytes 524288 | tf_op jit(solution)/shard_map/mul | solution.py:69
  153.4 6.0 %multiply_reduce_fusion.7 = f32[2,16,64]{2,1,0:T(8,128)S(1)} fusion(f32[2,16,8,64,8]{4,3,2,1,0:T(8,128)} %reshape.201, f32[16,8,64,8]{3,2,1,0:T(8,128)} %mul.219), kind=kLoop, calls=%fused_computation.7 | loop fusion | flops 260096 | bytes 794624 | tf_op jit(solution)/shard_map/reduce_sum | solution.py:70
  159.4 5.0 %multiply_reduce_fusion.6 = f32[2,16,64]{2,1,0:T(8,128)S(1)} fusion(f32[2,16,8,64,8]{4,3,2,1,0:T(8,128)} %reshape.202, f32[16,8,64,8]{3,2,1,0:T(8,128)S(1)} %copy-done.1), kind=kLoop, calls=%fused_computation.6 | loop fusion | flops 260096 | bytes 794624 | tf_op jit(solution)/shard_map/reduce_sum | solution.py:70
  164.5 5.0 %multiply_reduce_fusion.5 = f32[2,16,64]{2,1,0:T(8,128)S(1)} fusion(f32[2,16,8,64,8]{4,3,2,1,0:T(8,128)} %reshape.203, f32[16,8,64,8]{3,2,1,0:T(8,128)S(1)} %copy-done), kind=kLoop, calls=%fused_computation.5 | loop fusion | flops 260096 | bytes 794624 | tf_op jit(solution)/shard_map/reduce_sum | solution.py:70
  169.6 3.8 %multiply_reduce_fusion.4 = f32[2,16,64]{2,1,0:T(8,128)S(1)} fusion(f32[2,16,8,64,8]{4,3,2,1,0:T(8,128)S(1)} %bitcast.108, f32[16,8,64,8]{3,2,1,0:T(8,128)} %mul.231), kind=kLoop, calls=%fused_computation.4 | loop fusion | flops 260096 | bytes 794624 | tf_op jit(solution)/shard_map/reduce_sum | solution.py:70
  173.4 3.8 %multiply_reduce_fusion.3 = f32[2,16,64]{2,1,0:T(8,128)S(1)} fusion(f32[2,16,8,64,8]{4,3,2,1,0:T(8,128)S(1)} %bitcast.106, f32[16,8,64,8]{3,2,1,0:T(8,128)} %mul.235), kind=kLoop, calls=%fused_computation.3 | loop fusion | flops 260096 | bytes 794624 | tf_op jit(solution)/shard_map/reduce_sum | solution.py:70
  177.2 6.0 %multiply_reduce_fusion.2 = f32[2,16,64]{2,1,0:T(8,128)S(1)} fusion(f32[2,16,8,64,8]{4,3,2,1,0:T(8,128)} %reshape.206, f32[16,8,64,8]{3,2,1,0:T(8,128)} %mul.239), kind=kLoop, calls=%fused_computation.2 | loop fusion | flops 260096 | bytes 794624 | tf_op jit(solution)/shard_map/reduce_sum | solution.py:70
  183.2 3.8 %multiply_reduce_fusion.1 = f32[2,16,64]{2,1,0:T(8,128)S(1)} fusion(f32[2,16,8,64,8]{4,3,2,1,0:T(8,128)S(1)} %bitcast.104, f32[16,8,64,8]{3,2,1,0:T(8,128)} %mul.243), kind=kLoop, calls=%fused_computation.1 | loop fusion | flops 260096 | bytes 794624 | tf_op jit(solution)/shard_map/reduce_sum | solution.py:70
  190.6 7.5 %all-gather = f32[8,9,16,64]{3,2,0,1:T(8,128)S(1)} all-gather(f32[2,9,16,64]{3,2,0,1:T(8,128)S(1)} %constant_dynamic-update-slice_fusion), channel_id=2, replica_groups=mesh['layer'=4,'tx'=2,'ty'=4] {'layer'}, dimensions={0}, use_global_device_ids=true | all-gather | bytes 368640 | tf_op jit(solution)/shard_map/all_gather | solution.py:14
  (77 shorter events, 43.5 us)
Async XLA Ops:
  0.0 32.0 %copy-start.5 = (s32[1,9,2]{1,2,0:T(2,128)S(1)}, s32[1,9,2]{1,2,0:T(2,128)}, u32[]{:S(2)}) copy-start(s32[1,9,2]{1,2,0:T(2,128)} %param.7) | copy-start | bytes 220
  0.8 7.3 %collective-permute-start.1 = (f32[1,3,512]{2,1,0:T(4,128)S(1)}, f32[1,3,512]{2,1,0:T(4,128)S(1)}, u32[]{:S(2)}, u32[]{:S(2)}) collective-permute-start(f32[1,3,512]{2,1,0:T(4,128)S(1)} %get-tuple-element.33), channel_id=1, source_target_pairs={{4,0},{0,4},{5,1},{1,5},{6,2},{2,6},{7,3},{3,7},{12,8},{8,12},{13,... | collective-permute-start | bytes 18440 | tf_op jit(solution)/shard_map/ppermute | solution.py:30
  3.7 4.4 %collective-permute-start = (f32[1,3,512]{2,1,0:T(4,128)S(1)}, f32[1,3,512]{2,1,0:T(4,128)S(1)}, u32[]{:S(2)}, u32[]{:S(2)}) collective-permute-start(f32[1,3,512]{2,1,0:T(4,128)S(1)} %get-tuple-element.32), channel_id=1, source_target_pairs={{0,4},{4,0},{1,5},{5,1},{2,6},{6,2},{3,7},{7,3},{8,12},{12,8},{9,1... | collective-permute-start | bytes 18440 | tf_op jit(solution)/shard_map/ppermute | solution.py:28
  9.1 7.8 %collective-permute-start.3 = (f32[1,134,3]{2,1,0:T(8,128)S(1)}, f32[1,134,3]{2,1,0:T(8,128)S(1)}, u32[]{:S(2)}, u32[]{:S(2)}) collective-permute-start(f32[1,134,3]{2,1,0:T(8,128)S(1)} %get-tuple-element.29), channel_id=1, source_target_pairs={{1,0},{2,1},{3,2},{0,3},{5,4},{6,5},{7,6},{4,7},{9,8},{10,9},{11,1... | collective-permute-start | bytes 4832 | tf_op jit(solution)/shard_map/ppermute | solution.py:30
  13.2 6.1 %collective-permute-start.2 = (f32[1,134,3]{2,1,0:T(8,128)S(1)}, f32[1,134,3]{2,1,0:T(8,128)S(1)}, u32[]{:S(2)}, u32[]{:S(2)}) collective-permute-start(f32[1,134,3]{2,1,0:T(8,128)S(1)} %get-tuple-element.28), channel_id=1, source_target_pairs={{0,1},{1,2},{2,3},{3,0},{4,5},{5,6},{6,7},{7,4},{8,9},{9,10},{10,1... | collective-permute-start | bytes 4832 | tf_op jit(solution)/shard_map/ppermute | solution.py:28
  22.1 5.3 %collective-permute-start.5 = (f32[1,64,512]{2,1,0:T(8,128)S(1)}, f32[1,64,512]{2,1,0:T(8,128)S(1)}, u32[]{:S(2)}, u32[]{:S(2)}) collective-permute-start(f32[1,64,512]{2,1,0:T(8,128)S(1)} %get-tuple-element.31), channel_id=1, source_target_pairs={{4,0},{0,4},{5,1},{1,5},{6,2},{2,6},{7,3},{3,7},{12,8},{8,12},{13,... | collective-permute-start | bytes 393224 | tf_op jit(solution)/shard_map/ppermute | solution.py:30
  23.6 5.0 %collective-permute-start.4 = (f32[1,64,512]{2,1,0:T(8,128)S(1)}, f32[1,64,512]{2,1,0:T(8,128)S(1)}, u32[]{:S(2)}, u32[]{:S(2)}) collective-permute-start(f32[1,64,512]{2,1,0:T(8,128)S(1)} %get-tuple-element.30), channel_id=1, source_target_pairs={{0,4},{4,0},{1,5},{5,1},{2,6},{6,2},{3,7},{7,3},{8,12},{12,8},{9,1... | collective-permute-start | bytes 393224 | tf_op jit(solution)/shard_map/ppermute | solution.py:28
  28.6 0.7 copy-start.2
  30.0 82.5 %collective-permute-start.7 = (f32[1,256,64]{2,1,0:T(8,128)}, f32[1,256,64]{2,1,0:T(8,128)}, u32[]{:S(2)}, u32[]{:S(2)}) collective-permute-start(f32[1,256,64]{2,1,0:T(8,128)} %get-tuple-element.27), channel_id=1, source_target_pairs={{1,0},{2,1},{3,2},{0,3},{5,4},{6,5},{7,6},{4,7},{9,8},{10,9},{11,1... | collective-permute-start | bytes 196616 | tf_op jit(solution)/shard_map/ppermute | solution.py:30
  31.9 80.5 %collective-permute-start.6 = (f32[1,256,64]{2,1,0:T(8,128)}, f32[1,256,64]{2,1,0:T(8,128)}, u32[]{:S(2)}, u32[]{:S(2)}) collective-permute-start(f32[1,256,64]{2,1,0:T(8,128)} %get-tuple-element.26), channel_id=1, source_target_pairs={{0,1},{1,2},{2,3},{3,0},{4,5},{5,6},{6,7},{7,4},{8,9},{9,10},{10,1... | collective-permute-start | bytes 196616 | tf_op jit(solution)/shard_map/ppermute | solution.py:28
  100.2 12.2 %copy-start.3 = (f32[1,64,512]{2,1,0:T(8,128)S(1)}, f32[1,64,512]{2,1,0:T(8,128)}, u32[]{:S(2)}) copy-start(f32[1,64,512]{2,1,0:T(8,128)} %copy-done.2) | copy-start | bytes 393220
  100.2 13.5 %copy-start.4 = (s32[128,512]{1,0:T(8,128)S(1)}, s32[128,512]{1,0:T(8,128)}, u32[]{:S(2)}) copy-start(s32[128,512]{1,0:T(8,128)} %param.9) | copy-start | bytes 786436
  153.4 6.0 %copy-start.1 = (f32[16,8,64,8]{3,2,1,0:T(8,128)S(1)}, f32[16,8,64,8]{3,2,1,0:T(8,128)}, u32[]{:S(2)}) copy-start(f32[16,8,64,8]{3,2,1,0:T(8,128)} %mul.223) | copy-start | bytes 786436
  159.4 5.1 %copy-start = (f32[16,8,64,8]{3,2,1,0:T(8,128)S(1)}, f32[16,8,64,8]{3,2,1,0:T(8,128)}, u32[]{:S(2)}) copy-start(f32[16,8,64,8]{3,2,1,0:T(8,128)} %mul.227) | copy-start | bytes 786436
  159.4 10.1 %slice-start.6 = ((s8[8388608]{0:T(1024)(128)(4,1)}), s8[4194304]{0:T(1024)(128)(4,1)S(1)}, s32[]{:S(2)}) async-start(s8[8388608]{0:T(1024)(128)(4,1)} %bitcast.107), calls=%async_computation.6 | async-start | bytes 8388608
  164.5 5.1 %slice-start.7 = ((s8[8388608]{0:T(1024)(128)(4,1)}), s8[4194304]{0:T(1024)(128)(4,1)S(1)}, s32[]{:S(2)}) async-start(s8[8388608]{0:T(1024)(128)(4,1)} %bitcast.107), calls=%async_computation.7 | async-start | bytes 8388608
  164.5 8.9 %slice-start.4 = ((s8[8388608]{0:T(1024)(128)(4,1)}), s8[4194304]{0:T(1024)(128)(4,1)S(1)}, s32[]{:S(2)}) async-start(s8[8388608]{0:T(1024)(128)(4,1)} %bitcast.105), calls=%async_computation.4 | async-start | bytes 8388608
  169.5 3.8 %slice-start.5 = ((s8[8388608]{0:T(1024)(128)(4,1)}), s8[4194304]{0:T(1024)(128)(4,1)S(1)}, s32[]{:S(2)}) async-start(s8[8388608]{0:T(1024)(128)(4,1)} %bitcast.105), calls=%async_computation.5 | async-start | bytes 8388608
  173.4 9.8 %slice-start.2 = ((s8[8388608]{0:T(1024)(128)(4,1)}), s8[4194304]{0:T(1024)(128)(4,1)S(1)}, s32[]{:S(2)}) async-start(s8[8388608]{0:T(1024)(128)(4,1)} %bitcast.103), calls=%async_computation.2 | async-start | bytes 8388608
  177.1 6.1 %slice-start.3 = ((s8[8388608]{0:T(1024)(128)(4,1)}), s8[4194304]{0:T(1024)(128)(4,1)S(1)}, s32[]{:S(2)}) async-start(s8[8388608]{0:T(1024)(128)(4,1)} %bitcast.103), calls=%async_computation.3 | async-start | bytes 8388608
  177.1 9.9 %slice-start = ((s8[8388608]{0:T(1024)(128)(4,1)}), s8[4194304]{0:T(1024)(128)(4,1)S(1)}, s32[]{:S(2)}) async-start(s8[8388608]{0:T(1024)(128)(4,1)} %bitcast.101), calls=%async_computation | async-start | bytes 8388608
  183.2 3.8 %slice-start.1 = ((s8[8388608]{0:T(1024)(128)(4,1)}), s8[4194304]{0:T(1024)(128)(4,1)S(1)}, s32[]{:S(2)}) async-start(s8[8388608]{0:T(1024)(128)(4,1)} %bitcast.101), calls=%async_computation.1 | async-start | bytes 8388608
